TPU v7x, 32 devices: a whole 2x2x4 slice. The times are simulated.
32 devices in a mesh: dp: 16 (over z, x, core), tensor: 2 (over y).
Axes of the slice: x: 2, y: 2, z: 4, core: 2. Of those that a mesh axis runs over, the one named last changes fastest.
Arguments:
- layer_input: bfloat16 [16384, 1024], P('dp'), may hold values from -24 to 24
- amplitude: float32 [1024], replicated, may hold values from 0.5 to 1.5
- expansion: bfloat16 [1024, 2, 2048], P(None, None, 'tensor'), may hold values from -0.1875 to 0.1875
- timescale: bfloat16 [1024, 32], P(None, 'tensor'), may hold values from -0.375 to 0.375
- selection: bfloat16 [1024, 2, 128], replicated, may hold values from -0.1875 to 0.1875
- smoothing: float32 [4, 2048], P(None, 'tensor'), may hold values from -3 to 3
- baseline: float32 [2048], P('tensor'), may hold values from -3 to 3
- blending: float32 [4, 2, 128], replicated, may hold values from -3 to 3
- pedestal: float32 [2, 128], replicated, may hold values from -3 to 3
- offset: float32 [32], P('tensor'), may hold values from -6.9 to -2.3
- retention: float32 [32], P('tensor'), may hold values from 0 to 2.77
- passthrough: float32 [32], P('tensor'), may hold values from 0.1 to 1.9
- emphasis: float32 [2048], P('tensor'), may hold values from 0.5 to 1.5
- readout: bfloat16 [2048, 1024], P('tensor'), may hold values from -0.125 to 0.125
- cotangent: bfloat16 [16384, 1024], P('dp'), may hold values from -6 to 6
Outputs:
- layer_output: bfloat16 [16384, 1024], P('dp')
- input_gradient: bfloat16 [16384, 1024], P('dp')
- amplitude_gradient: float32 [1024], replicated
- expansion_gradient: float32 [1024, 2, 2048], P(None, None, 'tensor')
- timescale_gradient: float32 [1024, 32], P(None, 'tensor')
- selection_gradient: float32 [1024, 2, 128], replicated
- smoothing_gradient: float32 [4, 2048], P(None, 'tensor')
- baseline_gradient: float32 [2048], P('tensor')
- blending_gradient: float32 [4, 2, 128], replicated
- pedestal_gradient: float32 [2, 128], replicated
- offset_gradient: float32 [32], P('tensor')
- retention_gradient: float32 [32], P('tensor')
- passthrough_gradient: float32 [32], P('tensor')
- emphasis_gradient: float32 [2048], P('tensor')
- readout_gradient: float32 [2048, 1024], P('tensor')
All inputs are finite; a program needn't handle non-finite values.
Results may differ from a plain program's by a relative error of at most 0.025.
Values may be sent and summed in bfloat16 or wider, within the bound.
A program may use at most 192 MiB of HBM per device.

v0:
```python
import jax
import jax.numpy as jnp
from jax import lax
from jax.sharding import PartitionSpec as P

NH = 32
HEAD = 64
STATE = 128
SPAN = 256
KCONV = 4
LEN = 1024


epsilon = 1e-05


def for_sending(value):

    def short(part):
        return part.astype(jnp.bfloat16) if part.dtype == jnp.float32 else part

    return jax.tree.map(short, value)


def input_norm(values, amplitude):
    variance = jnp.mean(values * values, axis=-1, keepdims=True)
    return values * lax.rsqrt(variance + epsilon) * amplitude


def causal_conv(values, kernel, shift_term):
    length = values.shape[1]
    padded = jnp.pad(values, [(0, 0), (KCONV - 1, 0)] + [(0, 0)] * (values.ndim - 2))
    summed = shift_term + kernel[0] * padded[:, 0:length]
    for tap_index in range(1, KCONV):
        summed = summed + kernel[tap_index] * padded[:, tap_index : tap_index + length]
    return jax.nn.silu(summed)


def step_terms(raw_step, offset, retention):
    timestep = jax.nn.softplus(raw_step + offset)
    return (timestep, -timestep * jnp.exp(retention))


def gate_product(mixed, gate_values):
    return mixed * jax.nn.silu(gate_values)


def span_terms(scores, log_decay, timestep):
    cumulative = jnp.cumsum(log_decay, axis=-2)
    length = log_decay.shape[-2]
    causal = (jnp.arange(length)[:, None] >= jnp.arange(length)[None, :])[:, :, None]
    spread = cumulative[..., :, None, :] - cumulative[..., None, :, :]
    decay_factor = jnp.where(causal, jnp.exp(jnp.where(causal, spread, 0.0)), 0.0)
    mixing = scores[..., None] * decay_factor * timestep[..., None, :, :]
    growth = jnp.exp(cumulative)
    block_end = cumulative[..., -1:, :]
    weights_in = jnp.exp(block_end - cumulative) * timestep
    carried = jnp.exp(block_end[..., 0, :])
    return (mixing, growth, weights_in, carried)


def to_blocks(values, sequences, spans):
    shaped = values.reshape((sequences, spans, SPAN) + values.shape[2:])
    return jnp.moveaxis(shaped, 1, 0)


def from_blocks(values, row_count):
    return jnp.moveaxis(values, 0, 1).reshape((row_count,) + values.shape[3:])


def forward_block(carry_state, pieces):
    inner_block, select_block, decay_block, step_block = pieces
    input_map = select_block[:, :, 0]
    output_map = select_block[:, :, 1]
    scores = jnp.einsum("stn,sun->stu", output_map, input_map, preferred_element_type=jnp.float32)
    mixing, growth, weights_in, carried = span_terms(scores, decay_block, step_block)
    diagonal_term = jnp.einsum(
        "stuh,suhp->sthp",
        mixing.astype(jnp.bfloat16),
        inner_block,
        preferred_element_type=jnp.float32,
    )
    readout_term = jnp.einsum(
        "stn,shnp->sthp",
        output_map,
        carry_state.astype(jnp.bfloat16),
        preferred_element_type=jnp.float32,
    )
    weighted = (inner_block.astype(jnp.float32) * weights_in[..., None]).astype(jnp.bfloat16)
    produced = jnp.einsum("sun,suhp->shnp", input_map, weighted, preferred_element_type=jnp.float32)
    next_state = carried[..., None, None] * carry_state + produced
    output = diagonal_term + growth[..., None] * readout_term
    return (next_state, (output, carry_state))


def backward_block(state_grad, pieces):
    inner_block, select_block, decay_block, step_block, carry_state, output_grad = pieces
    input_map = select_block[:, :, 0]
    output_map = select_block[:, :, 1]
    scores = jnp.einsum("stn,sun->stu", output_map, input_map, preferred_element_type=jnp.float32)
    (mixing, growth, weights_in, carried), terms_pullback = jax.vjp(
        span_terms, scores, decay_block, step_block
    )
    mixing_low = mixing.astype(jnp.bfloat16)
    state_low = carry_state.astype(jnp.bfloat16)
    inner_float = inner_block.astype(jnp.float32)
    readout_term = jnp.einsum(
        "stn,shnp->sthp", output_map, state_low, preferred_element_type=jnp.float32
    )
    weighted = (inner_float * weights_in[..., None]).astype(jnp.bfloat16)
    output_float = output_grad.astype(jnp.float32)
    mixing_grad = jnp.einsum(
        "sthp,suhp->stuh", output_grad, inner_block, preferred_element_type=jnp.float32
    )
    inner_grad = jnp.einsum(
        "stuh,sthp->suhp", mixing_low, output_grad, preferred_element_type=jnp.float32
    )
    readout_grad = (growth[..., None] * output_float).astype(jnp.bfloat16)
    growth_grad = jnp.sum(output_float * readout_term, axis=-1)
    output_map_grad = jnp.einsum(
        "sthp,shnp->stn", readout_grad, state_low, preferred_element_type=jnp.float32
    )
    entering_grad = jnp.einsum(
        "stn,sthp->shnp", output_map, readout_grad, preferred_element_type=jnp.float32
    )
    entering_grad = entering_grad + carried[..., None, None] * state_grad
    carried_grad = jnp.sum(state_grad * carry_state, axis=(2, 3))
    produced_low = state_grad.astype(jnp.bfloat16)
    input_map_grad = jnp.einsum(
        "suhp,shnp->sun", weighted, produced_low, preferred_element_type=jnp.float32
    )
    weighted_grad = jnp.einsum(
        "sun,shnp->suhp", input_map, produced_low, preferred_element_type=jnp.float32
    )
    inner_grad = inner_grad + weighted_grad * weights_in[..., None]
    weights_grad = jnp.sum(weighted_grad * inner_float, axis=-1)
    scores_grad, decay_grad, step_grad = terms_pullback(
        (mixing_grad, growth_grad, weights_grad, carried_grad)
    )
    scores_low = scores_grad.astype(jnp.bfloat16)
    output_map_grad = output_map_grad + jnp.einsum(
        "stu,sun->stn", scores_low, input_map, preferred_element_type=jnp.float32
    )
    input_map_grad = input_map_grad + jnp.einsum(
        "stu,stn->sun", scores_low, output_map, preferred_element_type=jnp.float32
    )
    select_grad = jnp.stack([input_map_grad, output_map_grad], axis=2)
    return (entering_grad, (inner_grad, select_grad, decay_grad, step_grad))


def shards(
    layer_input,
    amplitude,
    expansion,
    timescale,
    selection,
    smoothing,
    baseline,
    blending,
    pedestal,
    offset,
    retention,
    passthrough,
    emphasis,
    readout,
    cotangent,
):
    row_count = layer_input.shape[0]
    sequences = row_count // LEN
    spans = LEN // SPAN
    head_count = timescale.shape[1]
    channels = expansion.shape[2]
    residual = layer_input.astype(jnp.float32)
    upstream = cotangent.astype(jnp.float32)
    normed, norm_pullback = jax.vjp(input_norm, residual, amplitude)
    normed_low = normed.astype(jnp.bfloat16)
    gate_inner = jnp.einsum(
        "ld,dkc->lkc", normed_low, expansion, preferred_element_type=jnp.float32
    )
    raw_step = jnp.dot(normed_low, timescale, preferred_element_type=jnp.float32)
    raw_select = jnp.einsum(
        "ld,dkn->lkn", normed_low, selection, preferred_element_type=jnp.float32
    )
    inner_act, inner_pullback = jax.vjp(
        causal_conv, gate_inner[:, 1].reshape(sequences, LEN, channels), smoothing, baseline
    )
    select_act, select_pullback = jax.vjp(
        causal_conv, raw_select.reshape(sequences, LEN, 2, STATE), blending, pedestal
    )
    inner_low = inner_act.astype(jnp.bfloat16)
    select_low = select_act.astype(jnp.bfloat16)
    (timestep, log_decay), step_pullback = jax.vjp(step_terms, raw_step, offset, retention)
    inner_blocks = to_blocks(inner_low.reshape(sequences, LEN, head_count, HEAD), sequences, spans)
    select_blocks = to_blocks(select_low, sequences, spans)
    decay_blocks = to_blocks(log_decay.reshape(sequences, LEN, head_count), sequences, spans)
    step_blocks = to_blocks(timestep.reshape(sequences, LEN, head_count), sequences, spans)
    initial_state = jnp.zeros((sequences, head_count, STATE, HEAD), jnp.float32)
    final_state, (block_out, entering) = lax.scan(
        forward_block, initial_state, (inner_blocks, select_blocks, decay_blocks, step_blocks)
    )
    inner_float = inner_low.reshape(row_count, head_count, HEAD).astype(jnp.float32)
    mixed = from_blocks(block_out, row_count) + passthrough[:, None] * inner_float
    gated, gate_pullback = jax.vjp(
        gate_product, mixed.reshape(row_count, channels), gate_inner[:, 0]
    )
    squares = lax.psum(jnp.sum(gated * gated, axis=1), "tensor")
    inverse = lax.rsqrt(squares / (NH * HEAD) + epsilon)
    scaled_low = (gated * emphasis).astype(jnp.bfloat16)
    projected = lax.psum(
        jnp.dot(scaled_low, readout, preferred_element_type=jnp.float32).astype(jnp.bfloat16),
        "tensor",
    ).astype(jnp.float32)
    layer_output = (residual + inverse[:, None] * projected).astype(jnp.bfloat16)
    inverse_grad = jnp.sum(upstream * projected, axis=1)
    projected_low = (inverse[:, None] * upstream).astype(jnp.bfloat16)
    readout_part = jnp.einsum(
        "lc,ld->cd", scaled_low, projected_low, preferred_element_type=jnp.float32
    )
    scaled_grad = jnp.einsum(
        "ld,cd->lc", projected_low, readout, preferred_element_type=jnp.float32
    )
    emphasis_part = jnp.sum(scaled_grad * gated, axis=0)
    early_terms = (readout_part, emphasis_part)
    gated_grad = (
        scaled_grad * emphasis
        - (inverse_grad * inverse * inverse * inverse / (NH * HEAD))[:, None] * gated
    )
    mixed_grad, gate_grad = gate_pullback(gated_grad)
    mixed_low = mixed_grad.astype(jnp.bfloat16)
    mixed_float = mixed_low.astype(jnp.float32).reshape(row_count, head_count, HEAD)
    passthrough_part = jnp.sum(mixed_float * inner_float, axis=(0, 2))
    output_blocks = to_blocks(mixed_low.reshape(sequences, LEN, head_count, HEAD), sequences, spans)
    last_grad, (inner_grads, select_grads, decay_grads, step_grads) = lax.scan(
        backward_block,
        jnp.zeros_like(initial_state),
        (inner_blocks, select_blocks, decay_blocks, step_blocks, entering, output_blocks),
        reverse=True,
    )
    inner_total = from_blocks(inner_grads, row_count) + passthrough[:, None] * mixed_float
    select_partial = from_blocks(select_grads, row_count).reshape(sequences, LEN, 2, STATE)
    select_total = lax.psum(select_partial.astype(jnp.bfloat16), "tensor").astype(jnp.float32)
    raw_step_grad, offset_part, retention_part = step_pullback(
        (from_blocks(step_grads, row_count), from_blocks(decay_grads, row_count))
    )
    inner_in_grad, smoothing_part, baseline_part = inner_pullback(
        inner_total.reshape(sequences, LEN, channels)
    )
    raw_select_grad, blending_part, pedestal_part = select_pullback(select_total)
    inner_stack = jnp.stack([gate_grad, inner_in_grad.reshape(row_count, channels)], axis=1).astype(
        jnp.bfloat16
    )
    step_low = raw_step_grad.astype(jnp.bfloat16)
    select_grad_low = raw_select_grad.reshape(row_count, 2, STATE).astype(jnp.bfloat16)
    expansion_part = jnp.einsum(
        "ld,lkc->dkc", normed_low, inner_stack, preferred_element_type=jnp.float32
    )
    timescale_part = jnp.einsum(
        "ld,lh->dh", normed_low, step_low, preferred_element_type=jnp.float32
    )
    selection_part = jnp.einsum(
        "ld,lkn->dkn", normed_low, select_grad_low, preferred_element_type=jnp.float32
    )
    summed_terms = jnp.einsum(
        "lkc,dkc->ld", inner_stack, expansion, preferred_element_type=jnp.float32
    )
    summed_terms = summed_terms + jnp.einsum(
        "lh,dh->ld", step_low, timescale, preferred_element_type=jnp.float32
    )
    normed_grad = lax.psum(summed_terms.astype(jnp.bfloat16), "tensor").astype(jnp.float32)
    normed_grad = normed_grad + jnp.einsum(
        "lkn,dkn->ld", select_grad_low, selection, preferred_element_type=jnp.float32
    )
    input_part, amplitude_part = norm_pullback(normed_grad)
    input_gradient = (upstream + input_part).astype(jnp.bfloat16)
    later_terms = (
        amplitude_part,
        expansion_part,
        timescale_part,
        selection_part,
        smoothing_part,
        baseline_part,
        blending_part,
        pedestal_part,
        offset_part,
        retention_part,
        passthrough_part,
    )
    summed_all = jax.tree.map(
        lambda part: part.astype(jnp.float32),
        lax.psum(for_sending(later_terms + early_terms), "dp"),
    )
    return (
        layer_output,
        input_gradient,
        summed_all[0],
        summed_all[1],
        summed_all[2],
        summed_all[3],
        summed_all[4],
        summed_all[5],
        summed_all[6],
        summed_all[7],
        summed_all[8],
        summed_all[9],
        summed_all[10],
        summed_all[12],
        summed_all[11],
    )


def solution(mesh):
    return jax.shard_map(
        shards,
        mesh=mesh,
        in_specs=(
            P("dp", None),
            P(),
            P(None, None, "tensor"),
            P(None, "tensor"),
            P(),
            P(None, "tensor"),
            P("tensor"),
            P(),
            P(),
            P("tensor"),
            P("tensor"),
            P("tensor"),
            P("tensor"),
            P("tensor", None),
            P("dp", None),
        ),
        out_specs=(
            P("dp", None),
            P("dp", None),
            P(),
            P(None, None, "tensor"),
            P(None, "tensor"),
            P(),
            P(None, "tensor"),
            P("tensor"),
            P(),
            P(),
            P("tensor"),
            P("tensor"),
            P("tensor"),
            P("tensor"),
            P("tensor", None),
        ),
        check_vma=False,
    )
```

profile of v0, /device:TPU:0, one launch (start us, length us, event | category | flops | bytes accessed | tf_op | source)
XLA Modules:
  0.0 638.4 jit_solution(7896230076383984365)
XLA Ops:
  44.9 31.7 %while.38 = (s32[]{:T(128)}, f32[1,16,128,64]{2,3,1,0:T(8,128)S(1)}, f32[4,1,256,16,64]{2,4,3,1,0:T(8,128)}, f32[4,1,16,128,64]{3,4,2,1,0:T(8,128)}, f32[4,1,256...) while((s32[]{:T(128)}, ...), condition=%wide.region_4.5_spmd.clone, body=%wide.region_1.4_spmd.clone.sunk | while | flops 294068288 | bytes 9031825 | solution.py:198
  87.6 8.1 %copy.267 = f32[4,1,256,16,64]{4,3,2,0,1:T(8,128)} copy(f32[4,1,256,16,64]{2,4,3,1,0:T(8,128)} %get-tuple-element.297) | data formatting | bytes 8388608 | tf_op jit(solution)/shard_map/reshape;transpose | solution.py:68
  95.7 7.1 %fusion.115 = f32[4,256]{1,0:T(4,128)S(1)} fusion(f32[4,1,256,16,64]{2,0,4,3,1:T(4,128)} %squeeze.75, bf16[4,1,256,16,64]{2,0,4,3,1:T(4,128)(2,1)} %transpose_reshape_reshape.13, f32[4,1,256,16,64]{2,4,3,1,0:T(8,128)} %get-tuple-element.297, f32[16]{0:T(128)S(1)} %copy-done.71), kind=kLoop, calls=%fused_computation.210 | loop fusion | flops 10484736 | bytes 10489920 | tf_op jit(solution)/shard_map/reduce_sum | solution.py:206
  102.9 5.9 psum.119
  108.8 8.0 %reshape.917 = f32[1024,1024]{1,0:T(8,128)} reshape(f32[4,1,256,16,64]{4,3,2,0,1:T(8,128)} %copy.267) | data formatting | bytes 8388608 | tf_op jit(solution)/shard_map/reshape;transpose | solution.py:68
  116.9 9.1 %multiply_reduce_fusion.3 = (bf16[1024]{0:T(1024)(128)(2,1)}, f32[1024,1024]{1,0:T(8,128)S(1)}, f32[1024,1024]{1,0:T(8,128)}) fusion(f32[1024,2,1024]{2,0,1:T(8,128)} %copy-done.3, f32[1024,1024]{1,0:T(8,128)} %reshape.917, bf16[1,1024,1024]{2,1,0:T(8,128)(2,1)} %get-tuple-element.664, f32[1024]{0:T(1024)S(1)} %mul.813, ...), kind=kOutput, calls=%fused_computation.199 | convolution fusion | flops 2161114112 | bytes 23078912 | tf_op jit(solution)/shard_map/ld,cd->lc/dot_general | solution.py:219
  131.8 64.8 %all-reduce.26.cloned.1.call-done = bf16[1024,1024]{1,0:T(8,128)(2,1)} async-done(((bf16[1024,1024]{1,0:T(8,128)(2,1)}), bf16[1024,1024]{1,0:T(8,128)(2,1)}) %all-reduce.26.cloned.1.call-update) | async-done | bytes 2097168 | tf_op jit(solution)/shard_map/psum | solution.py:209
  200.0 9.1 %fusion.98 = (f32[1024]{0:T(1024)}, bf16[1024,1024]{1,0:T(8,128)(2,1)}, bf16[1024,1,1024]{2,0,1:T(8,128)(2,1)}) fusion(bf16[1,1024,1024]{2,1,0:T(8,128)(2,1)} %get-tuple-element.664, f32[1024,2,1024]{2,0,1:T(8,128)} %copy-done.3, f32[1024,1024]{1,0:T(8,128)} %copy-done.17, f32[1024]{0:T(1024)S(1)} %fusion.148, f32[1024,1024]{1,0:T(8,128)} %get-tuple-element.697, ...), kind=kLoop, calls=%fused_computation.171 | loop fusion | flops 24116224 | bytes 23085056 | tf_op jit(solution)/shard_map/reduce_sum | solution.py:231
  209.1 6.3 reshape.918
  215.4 5.8 copy.251
  226.1 111.2 %while.39 = (s32[]{:T(128)}, f32[1,16,128,64]{2,3,1,0:T(8,128)S(1)}, f32[4,1,256,16,64]{2,4,3,1,0:T(8,128)}, bf16[4,1,256,2,128]{4,2,3,1,0:T(8,128)(2,1)}, f32[4...) while((s32[]{:T(128)}, ...), condition=%wide.region_22.23_spmd.clone, body=%wide.region_9.22_spmd.clone.sunk | while | flops 683200704 | bytes 22944352 | solution.py:233
  337.3 8.1 %copy.270 = f32[4,1,256,16,64]{4,3,2,0,1:T(8,128)} copy(f32[4,1,256,16,64]{2,4,3,1,0:T(8,128)} %get-tuple-element.299) | data formatting | bytes 8388608 | tf_op jit(solution)/shard_map/reshape;transpose | solution.py:68
  345.4 7.9 %reshape.919 = f32[1024,1024]{1,0:T(8,128)} reshape(f32[4,1,256,16,64]{4,3,2,0,1:T(8,128)} %copy.270) | data formatting | bytes 8388608 | tf_op jit(solution)/shard_map/reshape;transpose | solution.py:68
  353.3 10.5 %multiply_reduce_fusion.6 = (f32[1024]{0:T(1024)S(1)}, f32[1024]{0:T(1024)S(1)}, f32[1024]{0:T(1024)S(1)}, bf16[1024]{0:T(1024)(128)(2,1)S(1)}, f32[1024]{0:T(1024)S(1)}, /*index=5*/f32[1,1024,1024]{2,1,0:T(8,128)S(1)}) fusion(f32[1,1024,1024]{2,1,0:T(8,128)} %copy-done.2, f32[1024,2,1024]{2,0,1:T(8,128)} %copy-done.3, ...), kind=kLoop, calls=%fused_computation.202 | loop fusion | flops 22014976 | bytes 23091200 | tf_op jit(solution)/shard_map/transpose(jvp())/reduce_sum | solution.py:35
  363.8 6.6 %broadcast_multiply_fusion = (f32[1,1024,1024]{2,1,0:T(8,128)}, f32[1,1024,1024]{2,1,0:T(8,128)}, f32[1,1024,1024]{2,1,0:T(8,128)}, f32[1,1024,1024]{2,1,0:T(8,128)}) fusion(f32[1,1024,1024]{2,1,0:T(8,128)S(1)} %get-tuple-element.661, f32[1024]{0:T(1024)S(1)} %bitcast.622, f32[1024]{0:T(1024)S(1)} %bitcast.618, f32[1024]{0:T(1024)S(1)} %bitcast.620, ...), kind=kLoop, calls=%fused_computation.227 | loop fusion | flops 4194304 | bytes 20987904 | tf_op jit(solution)/shard_map/transpose(jvp())/mul | solution.py:35
  371.5 8.2 %fusion.123 = bf16[1024,1,1024]{2,0,1:T(8,128)(2,1)S(1)} fusion(f32[1,1024,1024]{2,1,0:T(8,128)} %get-tuple-element.676, f32[1,1024,1024]{2,1,0:T(8,128)} %get-tuple-element.677, f32[1,1024,1024]{2,1,0:T(8,128)} %get-tuple-element.678, f32[1,1024,1024]{2,1,0:T(8,128)} %get-tuple-element.675), kind=kLoop, calls=%fused_computation.220 | loop fusion | flops 4194304 | bytes 18874368 | tf_op jit(solution)/shard_map/stack;reshape | solution.py:249
  387.1 6.2 convolution_convert_fusion
  393.3 6.8 %fusion.121 = bf16[1024,2,1024]{2,0,1:T(8,128)(2,1)} fusion(bf16[1024,1,1024]{2,0,1:T(8,128)(2,1)S(1)} %copy-done.24, bf16[1024,1,1024]{2,0,1:T(8,128)(2,1)S(1)} %copy-done.22, bf16[1024,1024]{1,0:T(8,128)(2,1)S(1)} %copy-done.12, f32[1024]{0:T(1024)S(1)} %copy-done.70, f32[1024]{0:T(1024)S(1)} %copy-done.54), kind=kOutput, calls=%fused_computation.218 | convolution fusion | flops 4309647360 | bytes 10493952 | tf_op jit(solution)/shard_map/ld,lkc->dkc/dot_general | solution.py:254
  400.1 61.2 %all-reduce.30.cloned.1.call-done = (bf16[1,1024,2,128]{3,1,2,0:T(8,128)(2,1)}, bf16[1024,1024]{1,0:T(8,128)(2,1)}) async-done(((bf16[1,1024,2,128]{3,1,2,0:T(8,128)(2,1)}, bf16[1024,1024]{1,0:T(8,128)(2,1)}), (bf16[1,1024,2,128]{3,1,2,0:T(8,128)(2,1)}, bf16[1024,1024]{1,0:T(8,128)(2,1)})) %all-reduce.30.cloned.1.call-update) | async-done | bytes 2621456 | tf_op jit(solution)/shard_map/psum | solution.py:241
  468.4 5.9 fusion.94
  474.3 64.6 %all-reduce.19 = (bf16[1024]{0:T(1024)(128)(2,1)S(1)}, bf16[1024,16]{0,1:T(8,128)(2,1)S(1)}, bf16[4,1024]{1,0:T(4,128)(2,1)S(1)}, bf16[1024]{0:T(1024)(128)(2,1)...) all-reduce(bf16[1024]{0:T(1024)(128)(2,1)S(1)} %get-tuple-element.5, ...), channel_id=1, replica_groups=mesh['dp'=16,'tensor'=2] {'dp'}, use_global_device_ids=true, to_apply=%region_27.28 | all-reduce | flops 24880 | bytes 99520 | tf_op jit(solution)/shard_map/psum | solution.py:290
  544.7 5.8 fusion.101
  550.4 65.5 %all-reduce.28.cloned.1.call-done = (bf16[1024,2,1024]{2,0,1:T(8,128)(2,1)}, bf16[1024,2,128]{2,0,1:T(8,128)(2,1)}, bf16[1024,1024]{1,0:T(8,128)(2,1)}) async-done(((bf16[1024,2,1024]{2,0,1:T(8,128)(2,1)}, bf16[1024,2,128]{2,0,1:T(8,128)(2,1)}, bf16[1024,1024]{1,0:T(8,128)(2,1)}), (bf16[1024,2,1024]{2,0,1:T(8,128)(2,1)}, bf16[1024,2,128]{2,0,1:T(8,128)(2,1)}, ...) | async-done | bytes 6815760 | tf_op jit(solution)/shard_map/psum | solution.py:290
  616.0 10.0 %copy.263 = f32[1024,2,1024]{2,1,0:T(2,128)} copy(bf16[1024,2,1024]{2,0,1:T(8,128)(2,1)} %get-tuple-element.645) | data formatting | bytes 12582912
  (620 shorter events, 230.2 us)
Async XLA Ops:
  7.2 109.7 %copy-start = (bf16[1024,1024]{1,0:T(8,128)(2,1)S(1)}, bf16[1024,1024]{1,0:T(8,128)(2,1)}, u32[]{:S(2)}) copy-start(bf16[1024,1024]{1,0:T(8,128)(2,1)} %param.32) | copy-start | bytes 6291460
  7.2 189.4 %all-reduce.26.cloned.1.call-start = ((), (), s32[]{:S(2)}) async-start(), calls=%async_computation | async-start | bytes 4194304 | tf_op jit(solution)/shard_map/psum | solution.py:209
  9.5 31.3 %copy-start.53 = (f32[1024]{0:T(1024)}, f32[1024]{0:T(1024)S(1)}, u32[]{:S(2)}) copy-start(f32[1024]{0:T(1024)S(1)} %fusion.149) | copy-start | bytes 12292
  116.9 82.7 %copy-start.38 = (f32[1024]{0:T(1024)}, f32[1024]{0:T(1024)S(1)}, u32[]{:S(2)}) copy-start(f32[1024]{0:T(1024)S(1)} %mul.813) | copy-start | bytes 12292
  116.9 11.1 %copy-start.67 = (f32[1024]{0:T(1024)S(1)}, f32[1024]{0:T(1024)}, u32[]{:S(2)}) copy-start(f32[1024]{0:T(1024)} %param.31) | copy-start | bytes 12292
  131.7 329.7 %all-reduce.30.cloned.1.call-start = ((), (), s32[]{:S(2)}) async-start(), calls=%async_computation.2 | async-start | bytes 5242880 | tf_op jit(solution)/shard_map/psum | solution.py:241
  226.1 9.9 %copy-start.15 = (bf16[4,1,256,2,128]{4,2,3,1,0:T(8,128)(2,1)}, bf16[4,1,256,2,128]{4,2,3,1,0:T(8,128)(2,1)S(1)}, u32[]{:S(2)}) copy-start(bf16[4,1,256,2,128]{4,2,3,1,0:T(8,128)(2,1)S(1)} %get-tuple-element.925) | copy-start | bytes 1572868 | tf_op jit(solution)/shard_map/while
  226.1 9.9 %copy-start.19 = (f32[4,1,256,16]{2,3,1,0:T(8,128)}, f32[4,1,256,16]{2,3,1,0:T(8,128)S(1)}, u32[]{:S(2)}) copy-start(f32[4,1,256,16]{2,3,1,0:T(8,128)S(1)} %get-tuple-element.926) | copy-start | bytes 196612 | tf_op jit(solution)/shard_map/while
  226.1 9.9 %copy-start.28 = (f32[4,1,256,16]{2,0,3,1:T(4,128)}, f32[4,1,256,16]{2,0,3,1:T(4,128)S(1)}, u32[]{:S(2)}) copy-start(f32[4,1,256,16]{2,0,3,1:T(4,128)S(1)} %get-tuple-element.923) | copy-start | bytes 196612 | tf_op jit(solution)/shard_map/while
  281.7 9.9 %copy-start.15 = (bf16[4,1,256,2,128]{4,2,3,1,0:T(8,128)(2,1)}, bf16[4,1,256,2,128]{4,2,3,1,0:T(8,128)(2,1)S(1)}, u32[]{:S(2)}) copy-start(bf16[4,1,256,2,128]{4,2,3,1,0:T(8,128)(2,1)S(1)} %get-tuple-element.925) | copy-start | bytes 1572868 | tf_op jit(solution)/shard_map/while
  353.3 10.5 %copy-start.41 = (f32[1,1024]{1,0:T(1,128)S(1)}, f32[1,1024]{1,0:T(1,128)}, u32[]{:S(2)}) copy-start(f32[1,1024]{1,0:T(1,128)} %copy-done.40) | copy-start | bytes 12292
  353.3 10.5 %copy-start.43 = (f32[1,1024]{1,0:T(1,128)S(1)}, f32[1,1024]{1,0:T(1,128)}, u32[]{:S(2)}) copy-start(f32[1,1024]{1,0:T(1,128)} %copy-done.42) | copy-start | bytes 12292
  353.3 10.5 %copy-start.45 = (f32[1,1024]{1,0:T(1,128)S(1)}, f32[1,1024]{1,0:T(1,128)}, u32[]{:S(2)}) copy-start(f32[1,1024]{1,0:T(1,128)} %copy-done.44) | copy-start | bytes 12292
  353.3 10.5 %copy-start.47 = (f32[1,1024]{1,0:T(1,128)S(1)}, f32[1,1024]{1,0:T(1,128)}, u32[]{:S(2)}) copy-start(f32[1,1024]{1,0:T(1,128)} %copy-done.46) | copy-start | bytes 12292
  386.7 229.2 %all-reduce.28.cloned.1.call-start = ((), (), s32[]{:S(2)}) async-start(), calls=%async_computation.1 | async-start | bytes 13631488 | tf_op jit(solution)/shard_map/psum | solution.py:290
  393.3 68.1 %copy-start.7 = (f32[1024,2,128]{2,0,1:T(8,128)S(1)}, f32[1024,2,128]{2,0,1:T(8,128)}, u32[]{:S(2)}) copy-start(f32[1024,2,128]{2,0,1:T(8,128)} %copy-done.6) | copy-start | bytes 3145732
  393.3 68.1 %copy-start.18 = (f32[1,1024,2,128]{3,1,2,0:T(8,128)S(1)}, f32[1,1024,2,128]{3,1,2,0:T(8,128)}, u32[]{:S(2)}) copy-start(f32[1,1024,2,128]{3,1,2,0:T(8,128)} %get-tuple-element.663) | copy-start | bytes 3145732
  400.1 63.2 %copy-start.59 = (f32[2,128]{1,0:T(2,128)S(1)}, f32[2,128]{1,0:T(2,128)}, u32[]{:S(2)}) copy-start(f32[2,128]{1,0:T(2,128)} %copy-done.58) | copy-start | bytes 3076
  400.1 63.2 %copy-start.61 = (f32[2,128]{1,0:T(2,128)S(1)}, f32[2,128]{1,0:T(2,128)}, u32[]{:S(2)}) copy-start(f32[2,128]{1,0:T(2,128)} %copy-done.60) | copy-start | bytes 3076
  400.1 63.2 %copy-start.63 = (f32[2,128]{1,0:T(2,128)S(1)}, f32[2,128]{1,0:T(2,128)}, u32[]{:S(2)}) copy-start(f32[2,128]{1,0:T(2,128)} %copy-done.62) | copy-start | bytes 3076
  400.1 63.2 %copy-start.65 = (f32[2,128]{1,0:T(2,128)S(1)}, f32[2,128]{1,0:T(2,128)}, u32[]{:S(2)}) copy-start(f32[2,128]{1,0:T(2,128)} %copy-done.64) | copy-start | bytes 3076
  468.4 76.2 %copy-start.49 = (f32[1024]{0:T(1024)S(1)}, f32[1024]{0:T(1024)}, u32[]{:S(2)}) copy-start(f32[1024]{0:T(1024)} %copy-done.48) | copy-start | bytes 12292
  468.4 76.2 %copy-start.9 = (bf16[1024,1024]{1,0:T(8,128)(2,1)S(1)}, bf16[1024,1024]{1,0:T(8,128)(2,1)}, u32[]{:S(2)}) copy-start(bf16[1024,1024]{1,0:T(8,128)(2,1)} %param.33) | copy-start | bytes 6291460
  616.0 15.7 %copy-start.1 = (bf16[1024,1024]{1,0:T(8,128)(2,1)S(1)}, bf16[1024,1024]{1,0:T(8,128)(2,1)}, u32[]{:S(2)}) copy-start(bf16[1024,1024]{1,0:T(8,128)(2,1)} %param.32) | copy-start | bytes 6291460
  (100 other events, 507.9 us)
Sparse Core Ops, SparseCore 0:
  131.8 64.6 all-reduce.25
  386.8 74.5 all-reduce.29
  466.9 148.9 all-reduce.27
where the time goes:
time: 647 us; the launch traced here: 638 us
  waiting for transfers between devices  192 us (30%)
  matrix products  135 us (21%)
  local copies, waits for them, and re-layouts  117 us (18%)
  other arithmetic  107 us (17%)
  blocking collectives  70.5 us (11%)
  between operations  14.9 us (2%)
    psum x1, waiting for transfers between devices, shards(): lax.psum(for_sending(later_terms + early_terms), 'dp')  65.5 us
    psum x1, waiting for transfers between devices, shards(): lax.psum(jnp.dot(scaled_low, readout, preferred_element_type=jnp.float32)...  64.8 us
    psum x1, blocking collectives, shards(): lax.psum(for_sending(later_terms + early_terms), 'dp')  64.6 us
    psum x1, waiting for transfers between devices, shards(): lax.psum(select_partial.astype(jnp.bfloat16), 'tensor').astype(jnp.float32)  61.2 us
    another operation x5, local copies, waits for them, and re-layouts, from_blocks(): return jnp.moveaxis(values, 0, 1).reshape((row_count,) + values.shape[3:])  32.3 us
    unnamed x146, local copies, waits for them, and re-layouts  26.4 us
    dot_general x4, matrix products, backward_block(): jnp.einsum('sthp,suhp->stuh', output_grad, inner_block, preferred_element...  19.6 us
    another operation x24, other arithmetic  15.1 us
  transfers between devices with their start and end apart: 3, of which 3 were waited for; matrix products, arithmetic and copies ran while one was open for 5% of the time, Pallas kernels for 0%

commit v1 on v0

v1 whole, which is shorter than its diff:
```python
import jax
import jax.numpy as jnp
from jax import lax
from jax.experimental import pallas as pl
from jax.experimental.pallas import tpu as pltpu
from jax.sharding import PartitionSpec as P

NH = 32
HEAD = 64
STATE = 128
SPAN = 256
KCONV = 4
LEN = 1024


epsilon = 1e-05


def input_norm(values, amplitude):
    variance = jnp.mean(values * values, axis=-1, keepdims=True)
    return values * lax.rsqrt(variance + epsilon) * amplitude


def causal_conv(values, kernel, shift_term):
    length = values.shape[1]
    padded = jnp.pad(values, [(0, 0), (KCONV - 1, 0)] + [(0, 0)] * (values.ndim - 2))
    summed = shift_term + kernel[0] * padded[:, 0:length]
    for tap_index in range(1, KCONV):
        summed = summed + kernel[tap_index] * padded[:, tap_index : tap_index + length]
    return jax.nn.silu(summed)


def step_terms(raw_step, offset, retention):
    timestep = jax.nn.softplus(raw_step + offset)
    return (timestep, -timestep * jnp.exp(retention))


VMEM_BYTES = 56 * 1024 * 1024


def mm(left, right, left_axis, right_axis):
    return lax.dot_general(
        left, right, (((left_axis,), (right_axis,)), ((), ())), preferred_element_type=jnp.float32
    )


def expand(per_head, spread_map):
    high = per_head.astype(jnp.bfloat16)
    low = (per_head - high.astype(jnp.float32)).astype(jnp.bfloat16)
    return mm(high, spread_map, 1, 0) + mm(low, spread_map, 1, 0)


def collect(per_channel, spread_map):
    high = per_channel.astype(jnp.bfloat16)
    low = (per_channel - high.astype(jnp.float32)).astype(jnp.bfloat16)
    return mm(high, spread_map, 1, 1) + mm(low, spread_map, 1, 1)


def sigmoid(values):
    return 1.0 / (1.0 + jnp.exp(-values))


def forward_kernel(
    spans,
    x_ref,
    z_ref,
    select_ref,
    cum_ref,
    step_ref,
    cum_row_ref,
    step_row_ref,
    channel_ref,
    spread_ref,
    readout_ref,
    cotangent_ref,
    pre_ref,
    mixed_ref,
    scaled_ref,
    entering_ref,
    back_ref,
    projected_ref,
    token_ref,
    padded,
    state,
):
    channels = x_ref.shape[1]
    heads = channels // HEAD
    step = pl.program_id(0)
    x = x_ref[...].astype(jnp.float32)

    @pl.when(lax.rem(step, spans) == 0)
    def _():
        state[...] = jnp.zeros_like(state)
        padded[0:8, :] = jnp.zeros((8, channels), jnp.float32)

    padded[8 : 8 + SPAN, :] = x
    pre = channel_ref[4:5, :] + channel_ref[3:4, :] * x
    for tap in range(KCONV - 1):
        pre = pre + channel_ref[tap : tap + 1, :] * padded[5 + tap : 5 + tap + SPAN, :]
    padded[0:8, :] = x[SPAN - 8 :, :]
    pre_low = pre.astype(jnp.bfloat16)
    pre_ref[...] = pre_low
    pre = pre_low.astype(jnp.float32)
    inner = (pre * sigmoid(pre)).astype(jnp.bfloat16)
    inner_float = inner.astype(jnp.float32)

    spread_map = spread_ref[...]
    input_map = select_ref[:, 0:STATE]
    output_map = select_ref[:, STATE:]
    cum = cum_ref[...]
    growth = expand(jnp.exp(cum), spread_map)
    weights_in = expand(jnp.exp(cum[SPAN - 1 :, :] - cum) * step_ref[...], spread_map)
    state_low = state[...].astype(jnp.bfloat16)
    entering_ref[...] = state_low
    mixed = growth * mm(output_map, state_low, 1, 0) + channel_ref[6:7, :] * inner_float
    weighted = (inner_float * weights_in).astype(jnp.bfloat16)
    state[...] = growth[SPAN - 1 :, :] * state[...] + mm(input_map, weighted, 0, 0)

    scores = mm(output_map, input_map, 1, 1)
    rows = lax.broadcasted_iota(jnp.int32, (SPAN, SPAN), 0)
    columns = lax.broadcasted_iota(jnp.int32, (SPAN, SPAN), 1)
    causal = rows >= columns
    first_half = lax.broadcasted_iota(jnp.int32, (1, 2 * HEAD), 1) < HEAD
    parts = []
    for pair in range(heads // 2):
        inner_pair = inner[:, pair * 2 * HEAD : (pair + 1) * 2 * HEAD]
        total = mixed[:, pair * 2 * HEAD : (pair + 1) * 2 * HEAD]
        for side in range(2):
            head = 2 * pair + side
            gap = cum[:, head : head + 1] - cum_row_ref[head : head + 1, :]
            decay = jnp.exp(jnp.where(causal, gap, -1e30))
            mixing = (scores * decay * step_row_ref[head : head + 1, :]).astype(jnp.bfloat16)
            keep = first_half if side == 0 else jnp.logical_not(first_half)
            own = jnp.where(keep, inner_pair, jnp.zeros_like(inner_pair))
            total = total + mm(mixing, own, 1, 0)
        parts.append(total)
    mixed = jnp.concatenate(parts, axis=1)
    mixed_ref[...] = mixed.astype(jnp.bfloat16)
    z = z_ref[...].astype(jnp.float32)
    gated = mixed * (z * sigmoid(z))
    scaled = (gated * channel_ref[5:6, :]).astype(jnp.bfloat16)
    scaled_ref[...] = scaled
    back = mm(cotangent_ref[...], readout_ref[...], 1, 1)
    back_ref[...] = back.astype(jnp.bfloat16)
    projected_ref[...] = mm(scaled, readout_ref[...], 1, 0).astype(jnp.bfloat16)
    token_ref[:, 0:1] = jnp.sum(gated * gated, axis=1, keepdims=True)
    token_ref[:, 1:2] = jnp.sum(scaled.astype(jnp.float32) * back, axis=1, keepdims=True)


def backward_kernel(
    spans,
    x_ref,
    z_ref,
    pre_ref,
    mixed_ref,
    back_ref,
    entering_ref,
    select_ref,
    cum_ref,
    step_ref,
    cum_row_ref,
    channel_ref,
    spread_ref,
    token_ref,
    x_grad_ref,
    select_grad_ref,
    head_ref,
    row_ref,
    carried_ref,
    sums_ref,
    padded,
    state_grad,
    scores_sum,
):
    channels = x_ref.shape[1]
    heads = channels // HEAD
    step = pl.program_id(0)

    @pl.when(step == 0)
    def _():
        sums_ref[...] = jnp.zeros_like(sums_ref)

    @pl.when(lax.rem(step, spans) == 0)
    def _():
        state_grad[...] = jnp.zeros_like(state_grad)
        padded[SPAN : SPAN + 8, :] = jnp.zeros((8, channels), jnp.float32)

    inverse = token_ref[:, 0:1]
    pull = token_ref[:, 1:2]
    head_ref[:, 3 * heads : 3 * heads + 1] = inverse
    z = z_ref[...].astype(jnp.float32)
    mixed = mixed_ref[...].astype(jnp.float32)
    z_sigmoid = sigmoid(z)
    z_silu = z * z_sigmoid
    gated = mixed * z_silu
    scaled_grad = inverse * back_ref[...].astype(jnp.float32)
    sums_ref[5:6, :] += jnp.sum(scaled_grad * gated, axis=0, keepdims=True)
    gated_grad = scaled_grad * channel_ref[5:6, :] - pull * gated
    mixed_grad = (gated_grad * z_silu).astype(jnp.bfloat16)
    grad_float = mixed_grad.astype(jnp.float32)

    pre = pre_ref[...].astype(jnp.float32)
    pre_sigmoid = sigmoid(pre)
    pre_silu = pre * pre_sigmoid
    inner = pre_silu.astype(jnp.bfloat16)
    inner_float = inner.astype(jnp.float32)
    sums_ref[6:7, :] += jnp.sum(grad_float * inner_float, axis=0, keepdims=True)

    spread_map = spread_ref[...]
    input_map = select_ref[:, 0:STATE]
    output_map = select_ref[:, STATE:]
    cum = cum_ref[...]
    growth = expand(jnp.exp(cum), spread_map)
    weights_in = expand(jnp.exp(cum[SPAN - 1 :, :] - cum) * step_ref[...], spread_map)
    state_low = entering_ref[...]
    weighted = (inner_float * weights_in).astype(jnp.bfloat16)
    grown = growth * grad_float
    readout_grad = grown.astype(jnp.bfloat16)
    head_ref[:, 0:heads] = collect(grown * mm(output_map, state_low, 1, 0), spread_map)
    output_map_grad = mm(readout_grad, state_low, 1, 1)
    produced = state_grad[...]
    produced_low = produced.astype(jnp.bfloat16)
    carried_ref[...] = jnp.broadcast_to(
        jnp.sum(produced * state_low.astype(jnp.float32), axis=0, keepdims=True), carried_ref.shape
    )
    input_map_grad = mm(weighted, produced_low, 1, 1)
    weighted_grad = mm(input_map, produced_low, 1, 0)
    head_ref[:, heads : 2 * heads] = collect(weighted_grad * inner_float, spread_map)
    state_grad[...] = growth[SPAN - 1 :, :] * produced + mm(output_map, readout_grad, 0, 0)
    inner_grad = weighted_grad * weights_in + channel_ref[6:7, :] * grad_float

    scores = mm(input_map, output_map, 1, 1)
    rows = lax.broadcasted_iota(jnp.int32, (SPAN, SPAN), 0)
    columns = lax.broadcasted_iota(jnp.int32, (SPAN, SPAN), 1)
    causal = columns >= rows
    first_half = lax.broadcasted_iota(jnp.int32, (1, 2 * HEAD), 1) < HEAD
    steps = step_ref[...]
    parts = []
    for pair in range(heads // 2):
        lanes = slice(pair * 2 * HEAD, (pair + 1) * 2 * HEAD)
        inner_pair = inner[:, lanes]
        grad_pair = mixed_grad[:, lanes]
        total = inner_grad[:, lanes]
        for side in range(2):
            head = 2 * pair + side
            keep = first_half if side == 0 else jnp.logical_not(first_half)
            own = jnp.where(keep, grad_pair, jnp.zeros_like(grad_pair))
            mixing_grad = mm(inner_pair, own, 1, 1)
            gap = cum_row_ref[head : head + 1, :] - cum[:, head : head + 1]
            decay = jnp.exp(jnp.where(causal, gap, -1e30)) * steps[:, head : head + 1]
            total = total + mm((scores * decay).astype(jnp.bfloat16), own, 1, 0)
            reached = mixing_grad * decay
            if head == 0:
                scores_sum[...] = reached
            else:
                scores_sum[...] += reached
            flow = reached * scores
            row_ref[head : head + 1, :] = jnp.sum(flow, axis=0, keepdims=True)
            head_ref[:, 2 * heads + head : 2 * heads + head + 1] = jnp.sum(
                flow, axis=1, keepdims=True
            )
        parts.append(total)
    inner_grad = jnp.concatenate(parts, axis=1)
    scores_low = scores_sum[...].astype(jnp.bfloat16)
    select_grad_ref[:, 0:STATE] = input_map_grad + mm(scores_low, output_map, 1, 0)
    select_grad_ref[:, STATE:] = output_map_grad + mm(scores_low, input_map, 0, 0)

    pre_grad = inner_grad * (pre_sigmoid + pre_silu * (1.0 - pre_sigmoid))
    padded[0:SPAN, :] = pre_grad
    x = x_ref[...].astype(jnp.float32)
    x_grad = channel_ref[3:4, :] * pre_grad
    sums_ref[3:4, :] += jnp.sum(x * pre_grad, axis=0, keepdims=True)
    sums_ref[4:5, :] += jnp.sum(pre_grad, axis=0, keepdims=True)
    for tap in range(KCONV - 1):
        shifted = padded[3 - tap : 3 - tap + SPAN, :]
        x_grad = x_grad + channel_ref[tap : tap + 1, :] * shifted
        sums_ref[tap : tap + 1, :] += jnp.sum(x * shifted, axis=0, keepdims=True)
    x_grad_ref[...] = x_grad.astype(jnp.bfloat16)
    padded[SPAN : SPAN + 8, :] = pre_grad[0:8, :]


def swap_sum(part):
    if lax.axis_size("tensor") == 2:
        other = lax.ppermute(part, "tensor", [(0, 1), (1, 0)])
        return part.astype(jnp.float32) + other.astype(jnp.float32)
    return lax.psum(part, "tensor").astype(jnp.float32)


def in_blocks(values):
    return values.reshape((-1, SPAN) + values.shape[1:])


def shards(
    layer_input,
    amplitude,
    expansion,
    timescale,
    selection,
    smoothing,
    baseline,
    blending,
    pedestal,
    offset,
    retention,
    passthrough,
    emphasis,
    readout,
    cotangent,
):
    low = jnp.bfloat16
    wide = jnp.float32
    row_count, width = layer_input.shape
    sequences = row_count // LEN
    spans = LEN // SPAN
    blocks = row_count // SPAN
    heads = timescale.shape[1]
    channels = expansion.shape[2]
    residual = layer_input.astype(wide)
    upstream = cotangent.astype(wide)
    inverse_in = lax.rsqrt(jnp.mean(residual * residual, axis=1, keepdims=True) + epsilon)
    normed = (residual * inverse_in * amplitude).astype(low)
    expand_z = expansion[:, 0]
    expand_x = expansion[:, 1]
    select_map = selection.reshape(width, 2 * STATE)
    gate_inner = jnp.einsum(
        "ld,dkc->klc", normed, expansion, preferred_element_type=wide
    ).astype(low)
    z = gate_inner[0]
    raw_step = mm(normed, timescale, 1, 0)
    raw_select = mm(normed, select_map, 1, 0)
    select_act, select_pullback = jax.vjp(
        causal_conv,
        raw_select.reshape(sequences, LEN, 2 * STATE),
        blending.reshape(KCONV, 2 * STATE),
        pedestal.reshape(2 * STATE),
    )
    select_low = select_act.astype(low).reshape(row_count, 2 * STATE)
    (timestep, log_decay), step_pullback = jax.vjp(step_terms, raw_step, offset, retention)
    order = jnp.arange(SPAN)
    up_to = (order[:, None] >= order[None, :]).astype(wide)
    cumulative = jnp.einsum(
        "tu,buh->bth", up_to, in_blocks(log_decay), precision=lax.Precision.HIGHEST
    ).reshape(row_count, heads)
    cumulative_rows = cumulative.T
    step_rows = timestep.T
    channel_rows = jnp.concatenate(
        [
            smoothing,
            baseline[None],
            emphasis[None],
            jnp.repeat(passthrough, HEAD)[None],
            jnp.zeros((1, channels), wide),
        ]
    )
    spread_map = jnp.repeat(jnp.eye(heads, dtype=low), HEAD, axis=1)

    def rows_at(columns):
        return pl.BlockSpec((SPAN, columns), lambda i: (i, 0))

    def whole(shape):
        return pl.BlockSpec(shape, lambda i: (0,) * len(shape))

    parameters = pltpu.CompilerParams(
        dimension_semantics=("arbitrary",), vmem_limit_bytes=VMEM_BYTES
    )
    pre, mixed, scaled, entering, back, projected_part, token_part = pl.pallas_call(
        lambda *refs: forward_kernel(spans, *refs),
        grid=(blocks,),
        in_specs=[
            pl.BlockSpec((None, SPAN, channels), lambda i: (1, i, 0)),
            pl.BlockSpec((None, SPAN, channels), lambda i: (0, i, 0)),
            rows_at(2 * STATE),
            rows_at(heads),
            rows_at(heads),
            pl.BlockSpec((heads, SPAN), lambda i: (0, i)),
            pl.BlockSpec((heads, SPAN), lambda i: (0, i)),
            whole((8, channels)),
            whole((heads, channels)),
            whole((channels, width)),
            rows_at(width),
        ],
        out_specs=[
            rows_at(channels),
            rows_at(channels),
            rows_at(channels),
            pl.BlockSpec((STATE, channels), lambda i: (i, 0)),
            rows_at(channels),
            rows_at(width),
            rows_at(2),
        ],
        out_shape=[
            jax.ShapeDtypeStruct((row_count, channels), low),
            jax.ShapeDtypeStruct((row_count, channels), low),
            jax.ShapeDtypeStruct((row_count, channels), low),
            jax.ShapeDtypeStruct((blocks * STATE, channels), low),
            jax.ShapeDtypeStruct((row_count, channels), low),
            jax.ShapeDtypeStruct((row_count, width), low),
            jax.ShapeDtypeStruct((row_count, 2), wide),
        ],
        scratch_shapes=[
            pltpu.VMEM((SPAN + 8, channels), wide),
            pltpu.VMEM((STATE, channels), wide),
        ],
        compiler_params=parameters,
        cost_estimate=pl.CostEstimate(
            flops=8 * row_count * channels * width, bytes_accessed=20 * row_count * width, transcendentals=0
        ),
    )(
        gate_inner, gate_inner, select_low, cumulative, timestep, cumulative_rows, step_rows,
        channel_rows, spread_map, readout, cotangent,
    )
    squares, inverse_grad = lax.psum((token_part[:, 0], token_part[:, 1]), "tensor")
    squares, inverse_grad, projected_part = lax.optimization_barrier(
        (squares, inverse_grad, projected_part)
    )
    inverse = lax.rsqrt(squares / (NH * HEAD) + epsilon)
    pull = inverse_grad * inverse * inverse * inverse / (NH * HEAD)
    projected = swap_sum(projected_part)
    readout_part = mm((scaled.astype(wide) * inverse[:, None]).astype(low), cotangent, 0, 0)
    z_wide = z.astype(wide)
    mixed_wide = mixed.astype(wide)
    z_sigmoid = sigmoid(z_wide)
    z_silu = z_wide * z_sigmoid
    gated_grad = (
        inverse[:, None] * back.astype(wide) * emphasis - pull[:, None] * mixed_wide * z_silu
    )
    gate_grad = (gated_grad * mixed_wide * (z_sigmoid + z_silu * (1.0 - z_sigmoid))).astype(low)
    readout_sum = lax.psum(readout_part.astype(low), "dp")
    z_part = mm(normed, gate_grad, 0, 0).astype(low)
    z_part, inverse, pull = lax.optimization_barrier((z_part, inverse, pull))

    def rows_back(columns):
        return pl.BlockSpec((SPAN, columns), lambda i: (blocks - 1 - i, 0))

    x_grad, select_grad, head_terms, flow_rows, carried_terms, channel_sums = (
        pl.pallas_call(
            lambda *refs: backward_kernel(spans, *refs),
            grid=(blocks,),
            in_specs=[
                pl.BlockSpec((None, SPAN, channels), lambda i: (1, blocks - 1 - i, 0)),
                pl.BlockSpec((None, SPAN, channels), lambda i: (0, blocks - 1 - i, 0)),
                rows_back(channels),
                rows_back(channels),
                rows_back(channels),
                pl.BlockSpec((STATE, channels), lambda i: (blocks - 1 - i, 0)),
                rows_back(2 * STATE),
                rows_back(heads),
                rows_back(heads),
                pl.BlockSpec((heads, SPAN), lambda i: (0, blocks - 1 - i)),
                whole((8, channels)),
                whole((heads, channels)),
                rows_back(2),
            ],
            out_specs=[
                rows_back(channels),
                rows_back(2 * STATE),
                rows_back(3 * heads + 1),
                pl.BlockSpec((heads, SPAN), lambda i: (0, blocks - 1 - i)),
                pl.BlockSpec((8, channels), lambda i: (blocks - 1 - i, 0)),
                whole((8, channels)),
            ],
            out_shape=[
                jax.ShapeDtypeStruct((row_count, channels), low),
                jax.ShapeDtypeStruct((row_count, 2 * STATE), wide),
                jax.ShapeDtypeStruct((row_count, 3 * heads + 1), wide),
                jax.ShapeDtypeStruct((heads, row_count), wide),
                jax.ShapeDtypeStruct((blocks * 8, channels), wide),
                jax.ShapeDtypeStruct((8, channels), wide),
            ],
            scratch_shapes=[
                pltpu.VMEM((SPAN + 8, channels), wide),
                pltpu.VMEM((STATE, channels), wide),
                pltpu.VMEM((SPAN, SPAN), wide),
            ],
            compiler_params=parameters,
            cost_estimate=pl.CostEstimate(
                flops=2 * row_count * channels * width, bytes_accessed=2 * row_count * width, transcendentals=0
            ),
        )(
            gate_inner, gate_inner, pre, mixed, back, entering, select_low, cumulative, timestep,
            cumulative_rows, channel_rows, spread_map, jnp.stack([inverse, pull], axis=1),
        )
    )
    layer_output = (residual + head_terms[:, 3 * heads :] * projected).astype(low)
    x_grad, layer_output, readout_sum, z_part = lax.optimization_barrier(
        (x_grad, layer_output, readout_sum, z_part)
    )
    z_sum = lax.psum(z_part, "dp")
    cum_blocks = in_blocks(cumulative)
    step_blocks = in_blocks(timestep)
    growth_term, weights_grad, flow_in = (
        in_blocks(head_terms[:, i * heads : (i + 1) * heads]) for i in range(3)
    )
    flow_out = in_blocks(flow_rows.T)
    to_end = jnp.exp(cum_blocks[:, -1:] - cum_blocks)
    weights_term = weights_grad * to_end * step_blocks
    carried_grad = jnp.sum(
        carried_terms.reshape(blocks, 8, heads, HEAD)[:, 0], axis=2
    ) * jnp.exp(cum_blocks[:, -1])
    at_end = carried_grad + jnp.sum(weights_term, axis=1)
    cumulative_grad = flow_out - flow_in + growth_term - weights_term
    decay_grad = (
        jnp.einsum("ut,buh->bth", up_to, cumulative_grad, precision=lax.Precision.HIGHEST)
        + at_end[:, None]
    )
    safe_step = jnp.where(step_blocks > 0.0, step_blocks, 1.0)
    step_grad = flow_in / safe_step + weights_grad * to_end
    raw_step_grad, offset_part, retention_part = step_pullback(
        (step_grad.reshape(row_count, heads), decay_grad.reshape(row_count, heads))
    )
    raw_select_grad, blending_part, pedestal_part = select_pullback(
        select_grad.reshape(sequences, LEN, 2 * STATE)
    )
    step_low = raw_step_grad.astype(low)
    select_grad_low = raw_select_grad.reshape(row_count, 2 * STATE).astype(low)
    x_part = mm(normed, x_grad, 0, 0)
    normed_grad = (
        mm(gate_grad, expand_z, 1, 1)
        + mm(x_grad, expand_x, 1, 1)
        + mm(step_low, timescale, 1, 1)
        + mm(select_grad_low, select_map, 1, 1)
    )
    amplitude_part = jnp.sum(normed_grad * (residual * inverse_in), axis=0)
    normed_part = normed_grad.astype(low)
    time_rows = width * heads // channels
    head_row = jnp.concatenate(
        [offset_part, retention_part, jnp.zeros((channels - 2 * heads,), wide)]
    )[None]
    own_part = jnp.concatenate(
        [
            x_part,
            mm(normed, step_low, 0, 0).reshape(time_rows, channels),
            channel_sums,
            head_row,
        ]
    ).astype(low)
    shared_part = swap_sum(
        jnp.concatenate(
            [
                mm(normed, select_grad_low, 0, 0),
                blending_part,
                pedestal_part[None],
                amplitude_part.reshape(-1, 2 * STATE),
            ]
        ).astype(low)
    ).astype(low)
    own_part, shared_part, z_sum, normed_part = lax.optimization_barrier(
        (own_part, shared_part, z_sum, normed_part)
    )
    own_sum, shared_sum = jax.tree.map(
        lambda part: part.astype(wide), lax.psum((own_part, shared_part), "dp")
    )
    normed_grad = swap_sum(normed_part)
    scaled_back = normed_grad * amplitude
    input_gradient = (
        upstream
        + inverse_in * scaled_back
        - residual
        * (inverse_in * inverse_in * inverse_in)
        * jnp.mean(scaled_back * residual, axis=1, keepdims=True)
    ).astype(low)
    small = own_sum[width + time_rows :]
    return (
        layer_output,
        input_gradient,
        shared_sum[width + KCONV + 1 :].reshape(width),
        jnp.stack([z_sum.astype(wide), own_sum[:width]], axis=1),
        own_sum[width : width + time_rows].reshape(width, heads),
        shared_sum[:width].reshape(width, 2, STATE),
        small[0:KCONV],
        small[4],
        shared_sum[width : width + KCONV].reshape(KCONV, 2, STATE),
        shared_sum[width + KCONV].reshape(2, STATE),
        small[8, :heads],
        small[8, heads : 2 * heads],
        jnp.sum(small[6].reshape(heads, HEAD), axis=1),
        small[5],
        readout_sum.astype(wide),
    )


def solution(mesh):
    return jax.shard_map(
        shards,
        mesh=mesh,
        in_specs=(
            P("dp", None),
            P(),
            P(None, None, "tensor"),
            P(None, "tensor"),
            P(),
            P(None, "tensor"),
            P("tensor"),
            P(),
            P(),
            P("tensor"),
            P("tensor"),
            P("tensor"),
            P("tensor"),
            P("tensor", None),
            P("dp", None),
        ),
        out_specs=(
            P("dp", None),
            P("dp", None),
            P(),
            P(None, None, "tensor"),
            P(None, "tensor"),
            P(),
            P(None, "tensor"),
            P("tensor"),
            P(),
            P(),
            P("tensor"),
            P("tensor"),
            P("tensor"),
            P("tensor"),
            P("tensor", None),
        ),
        check_vma=False,
    )
```

time: 647 us -> 438 us (0.68)
  matrix products: 135 us -> 50 us
  local copies, waits for them, and re-layouts: 117 us -> 48.4 us
  blocking collectives: 70.5 us -> 6.38 us
  other arithmetic: 107 us -> 52.8 us
  Pallas kernels: 0 us -> 48.5 us
  waiting for transfers between devices: 192 us -> 203 us
    dot_general x56 -> x14, matrix products: 123 us -> 50 us  [the longest x11 40.4 us: mm(): lax.dot_general(left, right, (((left_axis,), (right_axis,)), ((), ())), p...]
    psum x2 -> x1, blocking collectives: 70.5 us -> 6.38 us  [shards(): lax.psum((token_part[:, 0], token_part[:, 1]), 'tensor')]
    another operation x74 -> x5, local copies, waits for them, and re-layouts: 56.7 us -> 3.79 us  [the longest x1 2.44 us: shards(): jnp.stack([z_sum.astype(wide), own_sum[:width]], axis=1)]
    pallas_call x0 -> x2, Pallas kernels: none -> 48.5 us  [the longest x1 27.9 us: shards(): pl.pallas_call(lambda *refs: backward_kernel(spans, *refs), grid=(blocks,...]
    reduce_sum x13 -> x5, other arithmetic: 26.7 us -> 8.33 us  [the longest x1 3.24 us: shards(): jnp.mean(scaled_back * residual, axis=1, keepdims=True)]
    another operation x25 -> x6, other arithmetic: 23.4 us -> 5.9 us  [the longest x2 5.86 us: shards(): jnp.stack([z_sum.astype(wide), own_sum[:width]], axis=1)]
    while x12 -> x0, matrix products: 12.5 us -> none
    reduce_sum x2 -> x1, other arithmetic: 12.4 us -> 2.16 us  [causal_conv(): kernel[tap_index] * padded[:, tap_index:tap_index + length]]
  transfers between devices with their start and end apart: 3 -> 6, of which waited for: 3 -> 4; matrix products, arithmetic and copies ran while one was open for 5% -> 23% of each run, Pallas kernels for 0% -> 7%
where the time goes in v1:
time: 438 us; the launch traced here: 429 us
  waiting for transfers between devices  203 us (46%)
  other arithmetic  52.8 us (12%)
  matrix products  50 us (11%)
  Pallas kernels  48.5 us (11%)
  local copies, waits for them, and re-layouts  48.4 us (11%)
  between operations  14.7 us (3%)
  blocking collectives  6.38 us (1%)
  starting transfers between devices  5.31 us (1%)
    psum x1, waiting for transfers between devices, shards(): lax.psum((own_part, shared_part), 'dp')  96.4 us
    psum x1, waiting for transfers between devices, shards(): z_sum = lax.psum(z_part, 'dp')  83.8 us
    dot_general x11, matrix products, mm(): lax.dot_general(left, right, (((left_axis,), (right_axis,)), ((), ())), p...  40.4 us
    pallas_call x1, Pallas kernels, shards(): pl.pallas_call(lambda *refs: backward_kernel(spans, *refs), grid=(blocks,...  27.9 us
    unnamed x72, local copies, waits for them, and re-layouts  21.3 us
    pallas_call x1, Pallas kernels, shards(): pl.pallas_call(lambda *refs: forward_kernel(spans, *refs), grid=(blocks,)...  20.5 us
    psum x1, waiting for transfers between devices, shards(): readout_sum = lax.psum(readout_part.astype(low), 'dp')  17.7 us
  transfers between devices with their start and end apart: 6, of which 4 were waited for; matrix products, arithmetic and copies ran while one was open for 23% of the time, Pallas kernels for 7%

profile of v1, /device:TPU:0, one launch (start us, length us, event | category | flops | bytes accessed | tf_op | source)
XLA Modules:
  0.0 429.2 jit_solution(9945736704948510041)
XLA Ops:
  21.1 8.5 %convert_bitcast_fusion.refs_0_.refs_1_ = bf16[2,1024,1024]{2,1,0:T(8,128)(2,1)} fusion(bf16[1024,1024]{1,0:T(8,128)(2,1)S(1)} %fusion.2, bf16[1024,2,1024]{2,1,0:T(2,128)(2,1)} %param.17), kind=kOutput, calls=%fused_computation.31 | convolution fusion | flops 4297064448 | bytes 10485760 | tf_op jit(solution)/shard_map/ld,dkc->klc/dot_general | solution.py:325
  33.1 20.5 %shard_map.262 = (bf16[1024,1024]{1,0:T(8,128)(2,1)}, bf16[1024,1024]{1,0:T(8,128)(2,1)}, bf16[1024,1024]{1,0:T(8,128)(2,1)}, bf16[512,1024]{1,0:T(8,128)(2,1)},...) custom-call(bf16[2,1024,1024]{2,1,0:T(8,128)(2,1)} %convert_bitcast_fusion.refs_0_.refs_1_, ...), custom_call_target="tpu_custom_call" | custom-call | flops 8589934592 | bytes 20971520 | tf_op jit(solution)/shard_map/pallas_call | solution.py:366
  55.3 6.4 %all-reduce.9 = (f32[1024]{0:T(1024)S(1)}, f32[1024]{0:T(1024)S(1)}) all-reduce(f32[1024]{0:T(1024)S(1)} %get-tuple-element.135, f32[1024]{0:T(1024)S(1)} %get-tuple-element.134), channel_id=1, replica_groups=mesh['dp'=16,'tensor'=2] {'tensor'}, use_global_device_ids=true, to_apply=%region_1.2 | all-reduce | flops 2048 | bytes 16384 | tf_op jit(solution)/shard_map/psum | solution.py:412
  61.8 6.2 %fusion.22 = bf16[1024,1024]{1,0:T(8,128)(2,1)} fusion(bf16[1024,1024]{1,0:T(8,128)(2,1)} %refs_10_.1, bf16[1024,1024]{1,0:T(8,128)(2,1)} %get-tuple-element.55, f32[1024]{0:T(1024)S(1)} %get-tuple-element.50), kind=kOutput, calls=%fused_computation.42 | convolution fusion | flops 2151677952 | bytes 6295552 | tf_op jit(solution)/shard_map/dot_general | solution.py:42
  71.2 4.5 %fusion.7 = bf16[1024,1024]{1,0:T(8,128)(2,1)S(1)} fusion(bf16[1024,1024]{1,0:T(8,128)(2,1)S(1)} %copy-done.6, bf16[1024,1024]{1,0:T(8,128)(2,1)} %get-tuple-element.44.refs_4_, bf16[2,1024,1024]{2,1,0:T(8,128)(2,1)} %convert_bitcast_fusion.refs_0_.refs_1_, f32[1024]{0:T(1024)S(1)} %get-tuple-element.51, f32[1024]{0:T(1024)S(1)} %copy-done.26, ...), kind=kLoop, calls=%fused_computation.17 | loop fusion | flops 18874368 | bytes 8400896 | tf_op jit(solution)/shard_map/convert_element_type | solution.py:427
  77.0 3.7 convolution_convert_fusion.1
  81.8 27.9 %shard_map.263 = (bf16[1024,1024]{1,0:T(8,128)(2,1)}, f32[1024,256]{1,0:T(8,128)}, f32[1024,49]{1,0:T(8,128)}, f32[16,1024]{1,0:T(8,128)}, f32[32,1024]{1,0:T(8,128)}, /*index=5*/f32[8,1024]{1,0:T(8,128)}) custom-call(bf16[2,1024,1024]{2,1,0:T(8,128)(2,1)} %convert_bitcast_fusion.refs_0_.refs_1_, bf16[2,1024,1024]{2,1,0:T(8,128)(2,1)} %convert_bitcast_fusion.refs_0_.refs_1_, ...), custom_call_target="tpu_custom_call" | custom-call | flops 2147483648 | bytes 2097152 | tf_op jit(solution)/shard_map/pallas_call | solution.py:436
  117.1 2.9 fusion.29
  129.8 2.8 fusion.54
  132.6 2.8 fusion.33
  135.4 3.2 copy.103
  139.2 6.8 %fusion.19 = f32[1024,1024]{1,0:T(8,128)} fusion(bf16[1024,1024]{1,0:T(8,128)(2,1)} %copy-done.17, bf16[1024,2,1024]{2,0,1:T(8,128)(2,1)} %copy.103), kind=kOutput, calls=%fused_computation.37 | convolution fusion | flops 2147483648 | bytes 8388608 | tf_op jit(solution)/shard_map/dot_general | solution.py:42
  145.9 4.1 fusion.12
  150.0 17.7 %all-reduce.15.cloned.1.call-done = bf16[1024,1024]{1,0:T(8,128)(2,1)} async-done(((bf16[1024,1024]{1,0:T(8,128)(2,1)}), bf16[1024,1024]{1,0:T(8,128)(2,1)}) %all-reduce.15.cloned.1.call-update) | async-done | bytes 2097168 | tf_op jit(solution)/shard_map/psum | solution.py:428
  167.7 9.9 %fusion.64 = (bf16[1024,1024]{1,0:T(8,128)(2,1)}, bf16[1024]{0:T(1024)(128)(2,1)S(1)}) fusion(f32[1024]{0:T(1024)S(1)} %get-tuple-element.166, bf16[1024,1024]{1,0:T(8,128)(2,1)S(1)} %copy-done.2, f32[1024,1024]{1,0:T(8,128)} %fusion.33, f32[1024,1024]{1,0:T(8,128)} %fusion.54, f32[1024,1024]{1,0:T(8,128)} %fusion.19, ...), kind=kOutput, calls=%fused_computation.143 | convolution fusion | flops 2155871232 | bytes 20977664 | tf_op jit(solution)/shard_map/dot_general | solution.py:42
  179.5 4.6 %convolution_convert_fusion = bf16[1024,1024]{1,0:T(8,128)(2,1)S(1)} fusion(bf16[1024,1024]{1,0:T(8,128)(2,1)} %copy-done.8, bf16[1024,1024]{1,0:T(8,128)(2,1)} %get-tuple-element.58), kind=kOutput, calls=%fused_computation.43 | convolution fusion | flops 2148532224 | bytes 6291456 | tf_op jit(solution)/shard_map/dot_general | solution.py:42
  185.6 5.3 %collective-permute-done.1 = bf16[1033,256]{1,0:T(8,128)(2,1)S(1)} collective-permute-done((bf16[1033,256]{1,0:T(8,128)(2,1)S(1)}, bf16[1033,256]{1,0:T(8,128)(2,1)S(1)}, u32[]{:S(2)}, u32[]{:S(2)}) %collective-permute-start.1) | collective-permute-done | bytes 528928 | tf_op jit(solution)/shard_map/ppermute | solution.py:284
  191.9 83.8 %all-reduce.17.cloned.1.call-done = bf16[1024,1024]{1,0:T(8,128)(2,1)} async-done(((bf16[1024,1024]{1,0:T(8,128)(2,1)}), bf16[1024,1024]{1,0:T(8,128)(2,1)}) %all-reduce.17.cloned.1.call-update) | async-done | bytes 2097168 | tf_op jit(solution)/shard_map/psum | solution.py:488
  277.3 4.1 convert_element_type.135
  283.8 96.4 %all-reduce.19.cloned.1.call-done = (bf16[1033,256]{1,0:T(8,128)(2,1)}, bf16[1049,1024]{1,0:T(8,128)(2,1)}) async-done(((bf16[1033,256]{1,0:T(8,128)(2,1)}, bf16[1049,1024]{1,0:T(8,128)(2,1)}), (bf16[1033,256]{1,0:T(8,128)(2,1)}, bf16[1049,1024]{1,0:T(8,128)(2,1)})) %all-reduce.19.cloned.1.call-update) | async-done | bytes 2677264 | tf_op jit(solution)/shard_map/psum | solution.py:551
  390.4 3.4 pad_maximum_fusion
  393.8 13.2 %copy.126 = f32[1024,2,1024]{2,1,0:T(2,128)} copy(f32[1024,2,1024]{2,0,1:T(8,128)S(1)} %pad_maximum_fusion) | data formatting | bytes 16777216
  415.0 3.2 fusion.16
  418.2 4.0 fusion.15
  (155 shorter events, 68.6 us)
Async XLA Ops:
  7.2 6.5 %copy-start = (bf16[1024,16]{0,1:T(8,128)(2,1)S(1)}, bf16[1024,16]{0,1:T(8,128)(2,1)}, u32[]{:S(2)}) copy-start(bf16[1024,16]{0,1:T(8,128)(2,1)} %param.18) | copy-start | bytes 98308
  7.2 160.5 %all-reduce.15.cloned.1.call-start = ((), (), s32[]{:S(2)}) async-start(), calls=%async_computation | async-start | bytes 4194304 | tf_op jit(solution)/shard_map/psum | solution.py:428
  13.0 8.1 %copy-start.8 = (bf16[1024,1024]{1,0:T(8,128)(2,1)}, bf16[1024,1024]{1,0:T(8,128)(2,1)S(1)}, u32[]{:S(2)}) copy-start(bf16[1024,1024]{1,0:T(8,128)(2,1)S(1)} %fusion.2) | copy-start | bytes 6291460
  16.1 13.5 %copy-start.20 = (f32[2,8,4,256]{3,1,2,0:T(8,128)}, f32[2,8,4,256]{3,1,2,0:T(8,128)S(1)}, u32[]{:S(2)}) copy-start(f32[2,8,4,256]{3,1,2,0:T(8,128)S(1)} %copy.132) | copy-start | bytes 196612
  21.1 9.3 %copy-start.30 = (f32[16]{0:T(128)S(1)}, f32[16]{0:T(128)}, u32[]{:S(2)}) copy-start(f32[16]{0:T(128)} %param.26) | copy-start | bytes 196
  21.1 9.5 %copy-start.26 = (f32[1024]{0:T(1024)S(1)}, f32[1024]{0:T(1024)}, u32[]{:S(2)}) copy-start(f32[1024]{0:T(1024)} %param.27) | copy-start | bytes 12292
  21.1 9.5 %copy-start.27 = (f32[4,1024]{1,0:T(4,128)S(1)}, f32[4,1024]{1,0:T(4,128)}, u32[]{:S(2)}) copy-start(f32[4,1024]{1,0:T(4,128)} %param.20) | copy-start | bytes 49156
  21.1 9.5 %copy-start.28 = (f32[1024]{0:T(1024)S(1)}, f32[1024]{0:T(1024)}, u32[]{:S(2)}) copy-start(f32[1024]{0:T(1024)} %param.21) | copy-start | bytes 12292
  21.1 10.1 %copy-start.29 = (f32[2,128]{1,0:T(2,128)S(1)}, f32[2,128]{1,0:T(2,128)}, u32[]{:S(2)}) copy-start(f32[2,128]{1,0:T(2,128)} %param.23) | copy-start | bytes 3076
  61.7 9.4 %copy-start.6 = (bf16[1024,1024]{1,0:T(8,128)(2,1)S(1)}, bf16[1024,1024]{1,0:T(8,128)(2,1)}, u32[]{:S(2)}) copy-start(bf16[1024,1024]{1,0:T(8,128)(2,1)} %get-tuple-element.43.refs_3_) | copy-start | bytes 6291460
  68.0 207.7 %all-reduce.17.cloned.1.call-start = ((), (), s32[]{:S(2)}) async-start(), calls=%async_computation.1 | async-start | bytes 4194304 | tf_op jit(solution)/shard_map/psum | solution.py:488
  68.0 77.9 %collective-permute-start = (bf16[1024,1024]{1,0:T(8,128)(2,1)}, bf16[1024,1024]{1,0:T(8,128)(2,1)}, u32[]{:S(2)}, u32[]{:S(2)}) collective-permute-start(bf16[1024,1024]{1,0:T(8,128)(2,1)} %get-tuple-element.54), channel_id=1, source_target_pairs={{0,1},{1,0},{2,3},{3,2},{4,5},{5,4},{6,7},{7,6},{8,9},{9,8},{10,11... | collective-permute-start | bytes 6291464 | tf_op jit(solution)/shard_map/ppermute | solution.py:284
  71.2 5.8 %copy-start.9 = (bf16[1024,1024]{1,0:T(8,128)(2,1)S(1)}, bf16[1024,1024]{1,0:T(8,128)(2,1)}, u32[]{:S(2)}) copy-start(bf16[1024,1024]{1,0:T(8,128)(2,1)} %copy-done.8) | copy-start | bytes 6291460
  81.8 27.9 %copy-start.13 = (f32[1,1024,256]{2,1,0:T(8,128)S(1)}, f32[1,1024,256]{2,1,0:T(8,128)}, u32[]{:S(2)}) copy-start(f32[1,1024,256]{2,1,0:T(8,128)} %get-tuple-element.146) | copy-start | bytes 3145732
  120.0 5.9 %copy-start.32 = (f32[16]{0:T(128)S(1)}, f32[16]{0:T(128)}, u32[]{:S(2)}) copy-start(f32[16]{0:T(128)} %param.25) | copy-start | bytes 196
  139.2 6.8 %copy-start.2 = (bf16[1024,1024]{1,0:T(8,128)(2,1)S(1)}, bf16[1024,1024]{1,0:T(8,128)(2,1)}, u32[]{:S(2)}) copy-start(bf16[1024,1024]{1,0:T(8,128)(2,1)} %param.15) | copy-start | bytes 6291460
  139.2 6.8 %copy-start.19 = (bf16[1024,1024]{1,0:T(8,128)(2,1)S(1)}, bf16[1024,1024]{1,0:T(8,128)(2,1)}, u32[]{:S(2)}) copy-start(bf16[1024,1024]{1,0:T(8,128)(2,1)} %get-tuple-element.54) | copy-start | bytes 6291460
  177.9 13.1 %collective-permute-start.1 = (bf16[1033,256]{1,0:T(8,128)(2,1)S(1)}, bf16[1033,256]{1,0:T(8,128)(2,1)S(1)}, u32[]{:S(2)}, u32[]{:S(2)}) collective-permute-start(bf16[1033,256]{1,0:T(8,128)(2,1)S(1)} %concatenate.18), channel_id=1, source_target_pairs={{0,1},{1,0},{2,3},{3,2},{4,5},{5,4},{6,7},{7,6},{8,9},{9,8},{10,11... | collective-permute-start | bytes 1586696 | tf_op jit(solution)/shard_map/ppermute | solution.py:284
  179.4 200.7 %all-reduce.19.cloned.1.call-start = ((), (), s32[]{:S(2)}) async-start(), calls=%async_computation.2 | async-start | bytes 5390336 | tf_op jit(solution)/shard_map/psum | solution.py:551
  275.7 139.2 %collective-permute-start.2 = (bf16[1024,1024]{1,0:T(8,128)(2,1)}, bf16[1024,1024]{1,0:T(8,128)(2,1)}, u32[]{:S(2)}, u32[]{:S(2)}) collective-permute-start(bf16[1024,1024]{1,0:T(8,128)(2,1)} %get-tuple-element.64), channel_id=1, source_target_pairs={{0,1},{1,0},{2,3},{3,2},{4,5},{5,4},{6,7},{7,6},{8,9},{9,8},{10,11... | collective-permute-start | bytes 6291464 | tf_op jit(solution)/shard_map/ppermute | solution.py:284
  384.0 23.0 %copy-start.4 = (f32[1049,1024]{1,0:T(8,128)}, f32[1049,1024]{1,0:T(8,128)S(1)}, u32[]{:S(2)}) copy-start(f32[1049,1024]{1,0:T(8,128)S(1)} %convert_element_type.134) | copy-start | bytes 12890116
  393.8 21.2 %copy-start.24 = (f32[1024]{0:T(1024)S(1)}, f32[1024]{0:T(1024)}, u32[]{:S(2)}) copy-start(f32[1024]{0:T(1024)} %param.16) | copy-start | bytes 12292
  412.1 6.1 %copy-start.3 = (bf16[1024,1024]{1,0:T(8,128)(2,1)S(1)}, bf16[1024,1024]{1,0:T(8,128)(2,1)}, u32[]{:S(2)}) copy-start(bf16[1024,1024]{1,0:T(8,128)(2,1)} %get-tuple-element.64) | copy-start | bytes 6291460
  412.1 6.1 %copy-start.16 = (bf16[1024,1024]{1,0:T(8,128)(2,1)S(1)}, bf16[1024,1024]{1,0:T(8,128)(2,1)}, u32[]{:S(2)}) copy-start(bf16[1024,1024]{1,0:T(8,128)(2,1)} %refs_10_.1) | copy-start | bytes 6291460
  (15 other events, 60.3 us)
Sparse Core Ops, SparseCore 0:
  68.1 99.5 all-reduce.14
  179.6 96.0 all-reduce.16
  280.0 100.1 all-reduce.18
